TPU v7x, 32 devices: a whole 2x2x4 slice. The times are simulated.
32 devices in a mesh: ctx: 8 (over y, x, core), tp: 4 (over z).
Axes of the slice: x: 2, y: 2, z: 4, core: 2. Of those that a mesh axis runs over, the one named last changes fastest.
Arguments:
- features: bfloat16 [2048, 3, 4096], P('ctx', None, 'tp'), may hold values from -6 to 6
- short_taps: float32 [3, 3, 4096], P(None, None, 'tp'), may hold values from -3.5 to 3.5
- residues: float32 [16, 256], P(None, 'tp'), may hold values from -1.5 to 1.5
- rates: float32 [16, 256], P(None, 'tp'), may hold values from 0.000146484375 to 0.05, as said below
- skip: float32 [4096], P('tp'), may hold values from -4 to 4
- out_weight: bfloat16 [4096, 4096], P(None, 'tp'), may hold values from -0.09375 to 0.09375
Outputs:
- mixed: bfloat16 [2048, 4096], P('ctx', 'tp')
Inputs may be any that keep to these rules, and one draw needn't show every extreme that they name: `rates`: decay rate of one mode of one filter.
All inputs are finite; a program needn't handle non-finite values.
Results may differ from a plain program's by a relative error of at most 0.0049.
Values may be sent and summed in bfloat16 or wider, within the bound.
A program may use at most 128 MiB of HBM per device.

v0:
```python
import functools

import jax
import jax.numpy as jnp
from jax import lax
from jax.experimental import pallas as pl
from jax.experimental.pallas import tpu as pltpu
from jax.sharding import PartitionSpec as P

MESH = pl.DeviceIdType.MESH
LANES = 128
SPAN = 64
HALO = 16


def iota(shape, dim):
    return lax.broadcasted_iota(jnp.int32, shape, dim)


def split(x):
    high = x.astype(jnp.bfloat16)
    low = (x - high.astype(jnp.float32)).astype(jnp.bfloat16)
    return high, low


def dot(left, right, dims):
    return lax.dot_general(
        left, right, ((dims[:1], dims[1:]), ((), ())), preferred_element_type=jnp.float32
    )


def kernel(
    n_ctx, n_tp, group,
    feats, taps, residues, rates, skip, w_hbm, out,
    halo, w, gath, prod, query, conv, states, rep_rates, row_rates, row_coefs,
    entering, e_send, e_recv, acc,
    w_sem, halo_sems, es_sems, er_sems, left_sems, right_sems, fwd_sems, recv_sems,
):
    me, z = lax.axis_index("ctx"), lax.axis_index("tp")
    rows, width = feats.shape[1], feats.shape[2]
    modes, filters = rates.shape
    blocks, chunks = width // LANES, rows // SPAN
    per = LANES // group

    w_copy = pltpu.make_async_copy(w_hbm, w, w_sem)
    w_copy.start()

    barrier = pltpu.get_barrier_semaphore()

    def greet(d, _):
        pl.semaphore_signal(
            barrier, inc=1, device_id=(lax.rem(me + d, n_ctx), z), device_id_type=MESH
        )
        return 0

    lax.fori_loop(1, n_ctx, greet, 0)

    @pl.when(z > 0)
    def _():
        pl.semaphore_signal(barrier, inc=1, device_id=(me, z - 1), device_id_type=MESH)

    @pl.when(z < n_tp - 1)
    def _():
        pl.semaphore_signal(barrier, inc=1, device_id=(me, z + 1), device_id_type=MESH)

    pick = (iota((filters, width), 0) == iota((filters, width), 1) // group).astype(jnp.float32)

    def repeat(x):
        return lax.dot_general(
            x, pick, (((1,), (0,)), ((), ())),
            precision=lax.Precision.HIGHEST, preferred_element_type=jnp.float32,
        )

    diag = iota((modes, width), 0) == iota((modes, width), 1) % modes
    rep_rates[...] = repeat(rates[...])
    row_rates[...] = jnp.sum(jnp.where(diag, rep_rates[...], 0.0), axis=0, keepdims=True)
    row_res = jnp.sum(jnp.where(diag, repeat(residues[...]), 0.0), axis=0, keepdims=True)
    row_coefs[...] = row_res * jnp.sqrt(2.0 * row_rates[...])

    neighbours = (z > 0).astype(jnp.int32) + (z < n_tp - 1).astype(jnp.int32)
    pl.semaphore_wait(barrier, n_ctx - 1 + neighbours)

    halo_copy = pltpu.make_async_remote_copy(
        src_ref=feats.at[:, pl.ds(rows - HALO, HALO), :],
        dst_ref=halo,
        send_sem=halo_sems.at[0],
        recv_sem=halo_sems.at[1],
        device_id=(lax.rem(me + 1, n_ctx), z),
        device_id_type=MESH,
    )

    @pl.when(me < n_ctx - 1)
    def _():
        halo_copy.start()

    @pl.when(me == 0)
    def _():
        halo[...] = jnp.zeros_like(halo)

    @pl.when(me > 0)
    def _():
        halo_copy.wait_recv()

    def lanes_of(b):
        return pl.ds(pl.multiple_of(b * LANES, LANES), LANES)

    def wide(x):
        return jnp.concatenate([x[k * SPAN : (k + 1) * SPAN] for k in range(chunks)], axis=1)

    def shorted(b, j):
        lanes = lanes_of(b)
        here = feats[j, :, lanes].astype(jnp.float32)
        before = halo[j, :, lanes].astype(jnp.float32)
        row = iota((rows, LANES), 0)
        last, second = before[HALO - 1 : HALO], before[HALO - 2 : HALO - 1]
        one = jnp.where(row == 0, last, pltpu.roll(here, 1, 0))
        two = jnp.where(row == 0, second, jnp.where(row == 1, last, pltpu.roll(here, 2, 0)))
        tap = [taps[s, pl.ds(j, 1), lanes] for s in range(3)]
        return tap[0] * here + tap[1] * one + tap[2] * two

    def first(b, _):
        lanes = lanes_of(b)
        query[b] = shorted(b, 0)
        product = shorted(b, 1) * shorted(b, 2)
        prod[b] = product
        rate = row_rates[:, lanes]
        left_over = (SPAN - iota((SPAN, LANES), 0)).astype(jnp.float32)
        high, low = split(jnp.exp(-rate * left_over))
        value = wide(product).astype(jnp.bfloat16)
        full = dot(high, value, (0, 0)) + dot(low, value, (0, 0))
        own = iota(full.shape, 0) // modes == (iota(full.shape, 1) % LANES) // group
        full = jnp.where(own, full, 0.0)
        state = full[:modes]
        for f in range(1, per):
            state = state + full[f * modes : (f + 1) * modes]
        states[b] = state
        decay = jnp.exp(-float(SPAN) * rep_rates[:, lanes])
        total = state[:, :LANES]
        for k in range(1, chunks):
            total = total * decay + state[:, k * LANES : (k + 1) * LANES]
        e_send[:, lanes] = total.astype(jnp.bfloat16)
        return 0

    lax.fori_loop(0, blocks, first, 0)

    def e_copy(d):
        return pltpu.make_async_remote_copy(
            src_ref=e_send,
            dst_ref=e_recv.at[d - 1],
            send_sem=es_sems.at[d - 1],
            recv_sem=er_sems.at[d - 1],
            device_id=(lax.rem(me + d, n_ctx), z),
            device_id_type=MESH,
        )

    def e_start(d, _):
        @pl.when(me + d < n_ctx)
        def _():
            e_copy(d).start()

        return 0

    lax.fori_loop(1, n_ctx, e_start, 0)

    def within(b, _):
        lanes = lanes_of(b)
        rate, coef = row_rates[:, lanes], row_coefs[:, lanes]
        at = iota((SPAN, LANES), 0).astype(jnp.float32)
        a_high, a_low = split(coef * jnp.exp(-rate * at))
        rise = jnp.exp(rate * at)
        rise_high = rise.astype(jnp.bfloat16).astype(jnp.float32)
        rise_low = rise - rise_high
        shape = (per * SPAN, LANES)
        own = iota(shape, 0) // SPAN == iota(shape, 1) // modes
        b_high = jnp.where(own, jnp.concatenate([rise_high] * per, 0), 0.0).astype(jnp.bfloat16)
        b_low = jnp.where(own, jnp.concatenate([rise_low] * per, 0), 0.0).astype(jnp.bfloat16)
        filt = (
            dot(a_high, b_high, (1, 1)) + dot(a_low, b_high, (1, 1)) + dot(a_high, b_low, (1, 1))
        )
        filt = jnp.where(
            iota(filt.shape, 0) >= iota(filt.shape, 1) % SPAN, filt, 0.0
        ).astype(jnp.bfloat16)
        value = jnp.concatenate([wide(prod[b])] * per, 0)
        own = iota(value.shape, 0) // SPAN == (iota(value.shape, 1) % LANES) // group
        value = jnp.where(own, value, 0.0).astype(jnp.bfloat16)
        conv[b] = dot(filt, value, (1, 0))
        return 0

    lax.fori_loop(0, blocks, within, 0)

    entering[...] = jnp.zeros_like(entering)

    def e_take(d, _):
        @pl.when(me >= d)
        def _():
            e_copy(d).wait_recv()
            span = ((d - 1) * rows).astype(jnp.float32)
            entering[...] += jnp.exp(-span * rep_rates[...]) * e_recv[d - 1].astype(jnp.float32)

        return 0

    lax.fori_loop(1, n_ctx, e_take, 0)

    def own_copy(b, to, sems):
        return pltpu.make_async_remote_copy(
            src_ref=gath.at[z, b],
            dst_ref=gath.at[z, b],
            send_sem=sems.at[b],
            recv_sem=recv_sems.at[z, b],
            device_id=(me, to),
            device_id_type=MESH,
        )

    def finish(b, _):
        lanes = lanes_of(b)
        rate, coef = row_rates[:, lanes], row_coefs[:, lanes]
        at = iota((SPAN, LANES), 0).astype(jnp.float32)
        a_high, a_low = split(coef * jnp.exp(-rate * at))
        decay = jnp.exp(-float(SPAN) * rep_rates[:, lanes])
        held, parts, state = entering[:, lanes], [], states[b]
        for k in range(chunks):
            parts.append(held)
            held = held * decay + state[:, k * LANES : (k + 1) * LANES]
        tall = jnp.concatenate([jnp.concatenate(parts, axis=1)] * per, 0)
        own = iota(tall.shape, 0) // modes == (iota(tall.shape, 1) % LANES) // group
        tall = jnp.where(own, tall, 0.0).astype(jnp.bfloat16)
        total = conv[b] + dot(a_high, tall, (1, 0)) + dot(a_low, tall, (1, 0))
        direct = skip[:, lanes]
        for k in range(chunks):
            span = pl.ds(k * SPAN, SPAN)
            value = total[:, k * LANES : (k + 1) * LANES] + direct * prod[b, span, :]
            gath[z, b, span, :] = (query[b, span, :] * value).astype(jnp.bfloat16)

        @pl.when(z > 0)
        def _():
            own_copy(b, z - 1, left_sems).start()

        @pl.when(z < n_tp - 1)
        def _():
            own_copy(b, z + 1, right_sems).start()

        return 0

    lax.fori_loop(0, blocks, finish, 0)

    def project(shard, p):
        left = jnp.concatenate([gath[shard, 2 * p], gath[shard, 2 * p + 1]], axis=1)
        depth = 2 * LANES
        at = pl.multiple_of(shard * width + p * depth, depth)
        acc[...] += dot(left, w[pl.ds(at, depth), :], (1, 0))

    w_copy.wait()
    acc[...] = jnp.zeros_like(acc)

    def own_step(p, _):
        project(z, p)
        return 0

    lax.fori_loop(0, blocks // 2, own_step, 0)

    def pass_copy(shard, b, to):
        return pltpu.make_async_remote_copy(
            src_ref=gath.at[shard, b],
            dst_ref=gath.at[shard, b],
            send_sem=fwd_sems.at[shard, b],
            recv_sem=recv_sems.at[shard, b],
            device_id=(me, to),
            device_id_type=MESH,
        )

    def hop(i, _):
        d, p = 1 + i // (blocks // 2), i % (blocks // 2)
        above, below = z + d, z - d
        for b in (2 * p, 2 * p + 1):
            @pl.when(above < n_tp)
            def _():
                pass_copy(above, b, lax.rem(z + 1, n_tp)).wait_recv()

                @pl.when(z > 0)
                def _():
                    pass_copy(above, b, z - 1).start()

            @pl.when(below >= 0)
            def _():
                pass_copy(below, b, lax.rem(z + 1, n_tp)).wait_recv()

                @pl.when(z < n_tp - 1)
                def _():
                    pass_copy(below, b, z + 1).start()

        @pl.when(above < n_tp)
        def _():
            project(above, p)

        @pl.when(below >= 0)
        def _():
            project(below, p)

        return 0

    lax.fori_loop(0, (n_tp - 1) * (blocks // 2), hop, 0)
    out[...] = acc[...].astype(out.dtype)

    @pl.when(me < n_ctx - 1)
    def _():
        halo_copy.wait_send()

    def e_sent(d, _):
        @pl.when(me + d < n_ctx)
        def _():
            e_copy(d).wait_send()

        return 0

    lax.fori_loop(1, n_ctx, e_sent, 0)

    def own_sent(b, _):
        @pl.when(z > 0)
        def _():
            own_copy(b, z - 1, left_sems).wait_send()

        @pl.when(z < n_tp - 1)
        def _():
            own_copy(b, z + 1, right_sems).wait_send()

        return 0

    lax.fori_loop(0, blocks, own_sent, 0)

    def pass_sent(i, _):
        shard, b = i // blocks, i % blocks

        @pl.when((shard > z) & (z > 0))
        def _():
            pass_copy(shard, b, z - 1).wait_send()

        @pl.when((shard < z) & (z < n_tp - 1))
        def _():
            pass_copy(shard, b, z + 1).wait_send()

        return 0

    lax.fori_loop(0, n_tp * blocks, pass_sent, 0)


def shards(n_ctx, n_tp, features, short_taps, residues, rates, skip, out_weight):
    rows, _, width = features.shape
    modes, filters = rates.shape
    group = width // filters
    blocks, chunks = width // LANES, rows // SPAN
    columns = out_weight.shape[1]
    vmem = pl.BlockSpec(memory_space=pltpu.VMEM)
    f32, bf16 = jnp.float32, jnp.bfloat16
    dma = pltpu.SemaphoreType.DMA
    return pl.pallas_call(
        functools.partial(kernel, n_ctx, n_tp, group),
        out_shape=jax.ShapeDtypeStruct((rows, columns), bf16),
        in_specs=[vmem] * 5 + [pl.BlockSpec(memory_space=pl.ANY)],
        out_specs=vmem,
        scratch_shapes=[
            pltpu.VMEM((3, HALO, width), bf16),
            pltpu.VMEM(out_weight.shape, bf16),
            pltpu.VMEM((n_tp, blocks, rows, LANES), bf16),
            pltpu.VMEM((blocks, rows, LANES), f32),
            pltpu.VMEM((blocks, rows, LANES), f32),
            pltpu.VMEM((blocks, SPAN, chunks * LANES), f32),
            pltpu.VMEM((blocks, modes, chunks * LANES), f32),
            pltpu.VMEM((modes, width), f32),
            pltpu.VMEM((1, width), f32),
            pltpu.VMEM((1, width), f32),
            pltpu.VMEM((modes, width), f32),
            pltpu.VMEM((modes, width), bf16),
            pltpu.VMEM((n_ctx - 1, modes, width), bf16),
            pltpu.VMEM((rows, columns), f32),
            dma(()),
            dma((2,)),
            dma((n_ctx - 1,)),
            dma((n_ctx - 1,)),
            dma((blocks,)),
            dma((blocks,)),
            dma((n_tp, blocks)),
            dma((n_tp, blocks)),
        ],
        compiler_params=pltpu.CompilerParams(
            collective_id=0, has_side_effects=True, vmem_limit_bytes=48 * 1024 * 1024
        ),
        cost_estimate=pl.CostEstimate(
            flops=2 * rows * width * n_tp * columns,
            bytes_accessed=2 * out_weight.size,
            transcendentals=0,
        ),
    )(
        jnp.transpose(features, (1, 0, 2)), short_taps, residues, rates,
        skip.reshape(1, width), out_weight,
    )


def solution(mesh):
    in_specs = (
        P("ctx", None, "tp"),
        P(None, None, "tp"),
        P(None, "tp"),
        P(None, "tp"),
        P("tp"),
        P(None, "tp"),
    )
    n_ctx, n_tp = mesh.shape["ctx"], mesh.shape["tp"]
    return jax.shard_map(
        functools.partial(shards, n_ctx, n_tp),
        mesh=mesh, in_specs=in_specs, out_specs=P("ctx", "tp"), check_vma=False,
    )
```

profile of v0, /device:TPU:4, one launch (start us, length us, event | category | flops | bytes accessed | tf_op | source)
XLA Modules:
  0.0 54.9 jit_solution(5608247133157605002)
XLA Ops:
  0.0 0.0 copy-start
  0.0 1.4 %copy-done = bf16[256,3,1024]{2,0,1:T(8,128)(2,1)S(1)} copy-done((bf16[256,3,1024]{2,0,1:T(8,128)(2,1)S(1)}, bf16[256,3,1024]{2,0,1:T(8,128)(2,1)}, u32[]{:S(2)}) %copy-start) | copy-done | bytes 1572888
  1.4 0.0 copy-start.1
  1.4 0.8 %copy-done.1 = f32[3,3,1024]{2,1,0:T(4,128)S(1)} copy-done((f32[3,3,1024]{2,1,0:T(4,128)S(1)}, f32[3,3,1024]{2,1,0:T(4,128)}, u32[]{:S(2)}) %copy-start.1) | copy-done | bytes 36888
  2.2 0.0 copy-start.2
  2.2 0.7 %copy-done.2 = f32[16,64]{1,0:T(8,128)S(1)} copy-done((f32[16,64]{1,0:T(8,128)S(1)}, f32[16,64]{1,0:T(8,128)}, u32[]{:S(2)}) %copy-start.2) | copy-done | bytes 4120
  2.9 0.0 copy-start.3
  2.9 0.7 %copy-done.3 = f32[16,64]{1,0:T(8,128)S(1)} copy-done((f32[16,64]{1,0:T(8,128)S(1)}, f32[16,64]{1,0:T(8,128)}, u32[]{:S(2)}) %copy-start.3) | copy-done | bytes 4120
  3.6 0.0 copy-start.4
  3.6 0.7 %copy-done.4 = f32[1024]{0:T(1024)S(1)} copy-done((f32[1024]{0:T(1024)S(1)}, f32[1024]{0:T(1024)}, u32[]{:S(2)}) %copy-start.4) | copy-done | bytes 4120
  4.3 49.8 %shard_map.64 = bf16[256,1024]{1,0:T(8,128)(2,1)S(1)} custom-call(bf16[3,256,1024]{2,1,0:T(8,128)(2,1)S(1)} %bitcast.2, f32[3,3,1024]{2,1,0:T(4,128)S(1)} %copy-done.1, f32[16,64]{1,0:T(8,128)S(1)} %copy-done.2, f32[16,64]{1,0:T(8,128)S(1)} %copy-done.3, f32[1,1024]{1,0:T(1,128)S(1)} %bitcast.3, bf16[4096,1024]{1,0:T(8,128)(2,1)} %w_hbm.1), custom_call_target="tpu_custom_call" | custom-call | flops 2147483648 | bytes 8388608 | tf_op jit(solution)/shard_map/pallas_call | solution.py:355
  54.1 0.8 %copy.8 = bf16[256,1024]{1,0:T(8,128)(2,1)} copy(bf16[256,1024]{1,0:T(8,128)(2,1)S(1)} %shard_map.64) | data formatting | bytes 1048576
Async XLA Ops:
  0.0 1.4 %copy-start = (bf16[256,3,1024]{2,0,1:T(8,128)(2,1)S(1)}, bf16[256,3,1024]{2,0,1:T(8,128)(2,1)}, u32[]{:S(2)}) copy-start(bf16[256,3,1024]{2,0,1:T(8,128)(2,1)} %param.6) | copy-start | bytes 4718596
  1.4 0.8 %copy-start.1 = (f32[3,3,1024]{2,1,0:T(4,128)S(1)}, f32[3,3,1024]{2,1,0:T(4,128)}, u32[]{:S(2)}) copy-start(f32[3,3,1024]{2,1,0:T(4,128)} %taps.1) | copy-start | bytes 110596
  2.2 0.7 %copy-start.2 = (f32[16,64]{1,0:T(8,128)S(1)}, f32[16,64]{1,0:T(8,128)}, u32[]{:S(2)}) copy-start(f32[16,64]{1,0:T(8,128)} %residues.1) | copy-start | bytes 12292
  2.9 0.7 %copy-start.3 = (f32[16,64]{1,0:T(8,128)S(1)}, f32[16,64]{1,0:T(8,128)}, u32[]{:S(2)}) copy-start(f32[16,64]{1,0:T(8,128)} %rates.1) | copy-start | bytes 12292
  3.6 0.7 %copy-start.4 = (f32[1024]{0:T(1024)S(1)}, f32[1024]{0:T(1024)}, u32[]{:S(2)}) copy-start(f32[1024]{0:T(1024)} %param.10) | copy-start | bytes 12292
where the time goes:
time: 55.2 us; the launch traced here: 54.9 us
  Pallas kernels  49.8 us (90%)
  local copies, waits for them, and re-layouts  5.08 us (9%)
    pallas_call x1, Pallas kernels, shards(): pl.pallas_call(functools.partial(kernel, n_ctx, n_tp, group), out_shape=j...  49.8 us
    unnamed x11, local copies, waits for them, and re-layouts  5.08 us

commit v1 on v0

--- a/solution.py
+++ b/solution.py
@@ -10,6 +10,7 @@
 MESH = pl.DeviceIdType.MESH
 LANES = 128
 SPAN = 64
+AHEAD = 3
 HALO = 16
 
 
@@ -31,10 +32,11 @@
 
 def kernel(
     n_ctx, n_tp, group,
-    feats, taps, residues, rates, skip, w_hbm, out,
-    halo, w, gath, prod, query, conv, states, rep_rates, row_rates, row_coefs,
+    feats_in, taps, residues, rates, skip, w_hbm, out,
+    feats,
+    halo, w, gath, prod, query, conv, filts, states, rep_rates, row_rates, row_coefs,
     entering, e_send, e_recv, acc,
-    w_sem, halo_sems, es_sems, er_sems, left_sems, right_sems, fwd_sems, recv_sems,
+    in_sem, w_sem, halo_sems, es_sems, er_sems, left_sems, right_sems, fwd_sems, recv_sems,
 ):
     me, z = lax.axis_index("ctx"), lax.axis_index("tp")
     rows, width = feats.shape[1], feats.shape[2]
@@ -42,6 +44,8 @@
     blocks, chunks = width // LANES, rows // SPAN
     per = LANES // group
 
+    load = pltpu.make_async_copy(feats_in, feats, in_sem)
+    load.start()
     w_copy = pltpu.make_async_copy(w_hbm, w, w_sem)
     w_copy.start()
 
@@ -81,7 +85,7 @@
     pl.semaphore_wait(barrier, n_ctx - 1 + neighbours)
 
     halo_copy = pltpu.make_async_remote_copy(
-        src_ref=feats.at[:, pl.ds(rows - HALO, HALO), :],
+        src_ref=feats_in.at[:, pl.ds(rows - HALO, HALO), :],
         dst_ref=halo,
         send_sem=halo_sems.at[0],
         recv_sem=halo_sems.at[1],
@@ -97,12 +101,35 @@
     def _():
         halo[...] = jnp.zeros_like(halo)
 
-    @pl.when(me > 0)
-    def _():
-        halo_copy.wait_recv()
-
     def lanes_of(b):
         return pl.ds(pl.multiple_of(b * LANES, LANES), LANES)
+
+    def filters_of(b, _):
+        lanes = lanes_of(b)
+        rate, coef = row_rates[:, lanes], row_coefs[:, lanes]
+        at = iota((SPAN, LANES), 0).astype(jnp.float32)
+        a_high, a_low = split(coef * jnp.exp(-rate * at))
+        rise = jnp.exp(rate * at)
+        rise_high = rise.astype(jnp.bfloat16).astype(jnp.float32)
+        rise_low = rise - rise_high
+        shape = (per * SPAN, LANES)
+        own = iota(shape, 0) // SPAN == iota(shape, 1) // modes
+        b_high = jnp.where(own, jnp.concatenate([rise_high] * per, 0), 0.0).astype(jnp.bfloat16)
+        b_low = jnp.where(own, jnp.concatenate([rise_low] * per, 0), 0.0).astype(jnp.bfloat16)
+        filt = (
+            dot(a_high, b_high, (1, 1)) + dot(a_low, b_high, (1, 1)) + dot(a_high, b_low, (1, 1))
+        )
+        filts[b] = jnp.where(
+            iota(filt.shape, 0) >= iota(filt.shape, 1) % SPAN, filt, 0.0
+        ).astype(jnp.bfloat16)
+        return 0
+
+    lax.fori_loop(0, blocks, filters_of, 0)
+    load.wait()
+
+    @pl.when(me > 0)
+    def _():
+        halo_copy.wait_recv()
 
     def wide(x):
         return jnp.concatenate([x[k * SPAN : (k + 1) * SPAN] for k in range(chunks)], axis=1)
@@ -163,30 +190,14 @@
     lax.fori_loop(1, n_ctx, e_start, 0)
 
     def within(b, _):
-        lanes = lanes_of(b)
-        rate, coef = row_rates[:, lanes], row_coefs[:, lanes]
-        at = iota((SPAN, LANES), 0).astype(jnp.float32)
-        a_high, a_low = split(coef * jnp.exp(-rate * at))
-        rise = jnp.exp(rate * at)
-        rise_high = rise.astype(jnp.bfloat16).astype(jnp.float32)
-        rise_low = rise - rise_high
-        shape = (per * SPAN, LANES)
-        own = iota(shape, 0) // SPAN == iota(shape, 1) // modes
-        b_high = jnp.where(own, jnp.concatenate([rise_high] * per, 0), 0.0).astype(jnp.bfloat16)
-        b_low = jnp.where(own, jnp.concatenate([rise_low] * per, 0), 0.0).astype(jnp.bfloat16)
-        filt = (
-            dot(a_high, b_high, (1, 1)) + dot(a_low, b_high, (1, 1)) + dot(a_high, b_low, (1, 1))
-        )
-        filt = jnp.where(
-            iota(filt.shape, 0) >= iota(filt.shape, 1) % SPAN, filt, 0.0
-        ).astype(jnp.bfloat16)
         value = jnp.concatenate([wide(prod[b])] * per, 0)
         own = iota(value.shape, 0) // SPAN == (iota(value.shape, 1) % LANES) // group
         value = jnp.where(own, value, 0.0).astype(jnp.bfloat16)
-        conv[b] = dot(filt, value, (1, 0))
-        return 0
-
-    lax.fori_loop(0, blocks, within, 0)
+        conv[b] = dot(filts[b], value, (1, 0))
+        return 0
+
+    ahead = min(AHEAD, blocks)
+    lax.fori_loop(0, ahead, within, 0)
 
     entering[...] = jnp.zeros_like(entering)
 
@@ -241,7 +252,13 @@
 
         return 0
 
-    lax.fori_loop(0, blocks, finish, 0)
+    def both(b, _):
+        finish(b, 0)
+        within(b + ahead, 0)
+        return 0
+
+    lax.fori_loop(0, blocks - ahead, both, 0)
+    lax.fori_loop(blocks - ahead, blocks, finish, 0)
 
     def project(shard, p):
         left = jnp.concatenate([gath[shard, 2 * p], gath[shard, 2 * p + 1]], axis=1)
@@ -355,15 +372,17 @@
     return pl.pallas_call(
         functools.partial(kernel, n_ctx, n_tp, group),
         out_shape=jax.ShapeDtypeStruct((rows, columns), bf16),
-        in_specs=[vmem] * 5 + [pl.BlockSpec(memory_space=pl.ANY)],
+        in_specs=[pl.BlockSpec(memory_space=pl.ANY)] + [vmem] * 4 + [pl.BlockSpec(memory_space=pl.ANY)],
         out_specs=vmem,
         scratch_shapes=[
+            pltpu.VMEM((3, rows, width), bf16),
             pltpu.VMEM((3, HALO, width), bf16),
             pltpu.VMEM(out_weight.shape, bf16),
             pltpu.VMEM((n_tp, blocks, rows, LANES), bf16),
             pltpu.VMEM((blocks, rows, LANES), f32),
             pltpu.VMEM((blocks, rows, LANES), f32),
             pltpu.VMEM((blocks, SPAN, chunks * LANES), f32),
+            pltpu.VMEM((blocks, SPAN, LANES // group * SPAN), bf16),
             pltpu.VMEM((blocks, modes, chunks * LANES), f32),
             pltpu.VMEM((modes, width), f32),
             pltpu.VMEM((1, width), f32),
@@ -372,6 +391,7 @@
             pltpu.VMEM((modes, width), bf16),
             pltpu.VMEM((n_ctx - 1, modes, width), bf16),
             pltpu.VMEM((rows, columns), f32),
+            dma(()),
             dma(()),
             dma((2,)),
             dma((n_ctx - 1,)),
@@ -382,7 +402,7 @@
             dma((n_tp, blocks)),
         ],
         compiler_params=pltpu.CompilerParams(
-            collective_id=0, has_side_effects=True, vmem_limit_bytes=48 * 1024 * 1024
+            collective_id=0, has_side_effects=True, vmem_limit_bytes=63 * 1024 * 1024
         ),
         cost_estimate=pl.CostEstimate(
             flops=2 * rows * width * n_tp * columns,

time: 55.2 us -> 54.1 us (0.980)
  local copies, waits for them, and re-layouts: 5.08 us -> 1.87 us
  Pallas kernels: 49.8 us -> 51.7 us
    unnamed x11 -> x1, local copies, waits for them, and re-layouts: 5.08 us -> 1.87 us
    pallas_call x1, Pallas kernels: 49.8 us -> 51.7 us  [shards(): pl.pallas_call(functools.partial(kernel, n_ctx, n_tp, group), out_shape=j...]
where the time goes in v1:
time: 54.1 us; the launch traced here: 53.6 us
  Pallas kernels  51.7 us (96%)
  local copies, waits for them, and re-layouts  1.87 us (3%)
    pallas_call x1, Pallas kernels, shards(): pl.pallas_call(functools.partial(kernel, n_ctx, n_tp, group), out_shape=j...  51.7 us
    unnamed x1, local copies, waits for them, and re-layouts  1.87 us

profile of v1, /device:TPU:4, one launch (start us, length us, event | category | flops | bytes accessed | tf_op | source)
XLA Modules:
  0.0 53.6 jit_solution(9448703112767776436)
XLA Ops:
  0.0 51.7 %shard_map.64 = bf16[256,1024]{1,0:T(8,128)(2,1)} custom-call(bf16[3,256,1024]{2,1,0:T(8,128)(2,1)} %bitcast.2, f32[3,3,1024]{2,1,0:T(4,128)} %taps.1, f32[16,64]{1,0:T(8,128)} %residues.1, f32[16,64]{1,0:T(8,128)} %rates.1, f32[1,1024]{1,0:T(1,128)} %bitcast.3, bf16[4096,1024]{1,0:T(8,128)(2,1)} %w_hbm.1), custom_call_target="tpu_custom_call" | custom-call | flops 2147483648 | bytes 8388608 | tf_op jit(solution)/shard_map/pallas_call | solution.py:372
  51.7 1.9 %copy.8 = bf16[256,1024]{1,0:T(8,128)(2,1)} copy(bf16[256,1024]{1,0:T(8,128)(2,1)} %shard_map.64) | data formatting | bytes 1048576

commit v2 on v1

--- a/solution.py
+++ b/solution.py
@@ -47,7 +47,6 @@
     load = pltpu.make_async_copy(feats_in, feats, in_sem)
     load.start()
     w_copy = pltpu.make_async_copy(w_hbm, w, w_sem)
-    w_copy.start()
 
     barrier = pltpu.get_barrier_semaphore()
 
@@ -124,8 +123,11 @@
         ).astype(jnp.bfloat16)
         return 0
 
-    lax.fori_loop(0, blocks, filters_of, 0)
+    ahead = min(AHEAD, blocks)
+    for b in range(ahead):
+        filters_of(b, 0)
     load.wait()
+    w_copy.start()
 
     @pl.when(me > 0)
     def _():
@@ -147,7 +149,6 @@
 
     def first(b, _):
         lanes = lanes_of(b)
-        query[b] = shorted(b, 0)
         product = shorted(b, 1) * shorted(b, 2)
         prod[b] = product
         rate = row_rates[:, lanes]
@@ -168,7 +169,8 @@
         e_send[:, lanes] = total.astype(jnp.bfloat16)
         return 0
 
-    lax.fori_loop(0, blocks, first, 0)
+    for b in range(blocks):
+        first(b, 0)
 
     def e_copy(d):
         return pltpu.make_async_remote_copy(
@@ -190,14 +192,15 @@
     lax.fori_loop(1, n_ctx, e_start, 0)
 
     def within(b, _):
+        query[b] = shorted(b, 0)
         value = jnp.concatenate([wide(prod[b])] * per, 0)
         own = iota(value.shape, 0) // SPAN == (iota(value.shape, 1) % LANES) // group
         value = jnp.where(own, value, 0.0).astype(jnp.bfloat16)
         conv[b] = dot(filts[b], value, (1, 0))
         return 0
 
-    ahead = min(AHEAD, blocks)
-    lax.fori_loop(0, ahead, within, 0)
+    for b in range(ahead):
+        within(b, 0)
 
     entering[...] = jnp.zeros_like(entering)
 
@@ -253,6 +256,7 @@
         return 0
 
     def both(b, _):
+        filters_of(b + ahead, 0)
         finish(b, 0)
         within(b + ahead, 0)
         return 0

time: 54.1 us -> 52.2 us (0.965)
  Pallas kernels: 51.7 us -> 50.1 us
    pallas_call x1, Pallas kernels: 51.7 us -> 50.1 us  [shards(): pl.pallas_call(functools.partial(kernel, n_ctx, n_tp, group), out_shape=j...]
where the time goes in v2:
time: 52.2 us; the launch traced here: 52 us
  Pallas kernels  50.1 us (96%)
  local copies, waits for them, and re-layouts  1.87 us (4%)
    pallas_call x1, Pallas kernels, shards(): pl.pallas_call(functools.partial(kernel, n_ctx, n_tp, group), out_shape=j...  50.1 us
    unnamed x1, local copies, waits for them, and re-layouts  1.87 us

profile of v2, /device:TPU:4, one launch (start us, length us, event | category | flops | bytes accessed | tf_op | source)
XLA Modules:
  0.0 52.0 jit_solution(12794087343514824857)
XLA Ops:
  0.0 50.1 %shard_map.64 = bf16[256,1024]{1,0:T(8,128)(2,1)} custom-call(bf16[3,256,1024]{2,1,0:T(8,128)(2,1)} %bitcast.2, f32[3,3,1024]{2,1,0:T(4,128)} %taps.1, f32[16,64]{1,0:T(8,128)} %residues.1, f32[16,64]{1,0:T(8,128)} %rates.1, f32[1,1024]{1,0:T(1,128)} %bitcast.3, bf16[4096,1024]{1,0:T(8,128)(2,1)} %w_hbm.1), custom_call_target="tpu_custom_call" | custom-call | flops 2147483648 | bytes 8388608 | tf_op jit(solution)/shard_map/pallas_call | solution.py:376
  50.1 1.9 %copy.8 = bf16[256,1024]{1,0:T(8,128)(2,1)} copy(bf16[256,1024]{1,0:T(8,128)(2,1)} %shard_map.64) | data formatting | bytes 1048576

commit v3 on v2

--- a/solution.py
+++ b/solution.py
@@ -277,8 +277,6 @@
         project(z, p)
         return 0
 
-    lax.fori_loop(0, blocks // 2, own_step, 0)
-
     def pass_copy(shard, b, to):
         return pltpu.make_async_remote_copy(
             src_ref=gath.at[shard, b],
@@ -319,7 +317,9 @@
 
         return 0
 
-    lax.fori_loop(0, (n_tp - 1) * (blocks // 2), hop, 0)
+    lax.fori_loop(0, blocks // 2, hop, 0)
+    lax.fori_loop(0, blocks // 2, own_step, 0)
+    lax.fori_loop(blocks // 2, (n_tp - 1) * (blocks // 2), hop, 0)
     out[...] = acc[...].astype(out.dtype)
 
     @pl.when(me < n_ctx - 1)

time: 52.2 us -> 52.2 us (level)
  no operation moved by 1% of the time
where the time goes in v3:
time: 52.2 us; the launch traced here: 52 us
  Pallas kernels  50.1 us (96%)
  local copies, waits for them, and re-layouts  1.87 us (4%)
    pallas_call x1, Pallas kernels, shards(): pl.pallas_call(functools.partial(kernel, n_ctx, n_tp, group), out_shape=j...  50.1 us
    unnamed x1, local copies, waits for them, and re-layouts  1.87 us

profile of v3, /device:TPU:4, one launch (start us, length us, event | category | flops | bytes accessed | tf_op | source)
XLA Modules:
  0.0 52.0 jit_solution(2896175876359662411)
XLA Ops:
  0.0 50.1 %shard_map.64 = bf16[256,1024]{1,0:T(8,128)(2,1)} custom-call(bf16[3,256,1024]{2,1,0:T(8,128)(2,1)} %bitcast.2, f32[3,3,1024]{2,1,0:T(4,128)} %taps.1, f32[16,64]{1,0:T(8,128)} %residues.1, f32[16,64]{1,0:T(8,128)} %rates.1, f32[1,1024]{1,0:T(1,128)} %bitcast.3, bf16[4096,1024]{1,0:T(8,128)(2,1)} %w_hbm.1), custom_call_target="tpu_custom_call" | custom-call | flops 2147483648 | bytes 8388608 | tf_op jit(solution)/shard_map/pallas_call | solution.py:376
  50.1 1.9 %copy.8 = bf16[256,1024]{1,0:T(8,128)(2,1)} copy(bf16[256,1024]{1,0:T(8,128)(2,1)} %shard_map.64) | data formatting | bytes 1048576

commit v4 on v3

--- a/solution.py
+++ b/solution.py
@@ -375,7 +375,7 @@
     dma = pltpu.SemaphoreType.DMA
     return pl.pallas_call(
         functools.partial(kernel, n_ctx, n_tp, group),
-        out_shape=jax.ShapeDtypeStruct((rows, columns), bf16),
+        out_shape=pltpu.VMEM((rows, columns), bf16),
         in_specs=[pl.BlockSpec(memory_space=pl.ANY)] + [vmem] * 4 + [pl.BlockSpec(memory_space=pl.ANY)],
         out_specs=vmem,
         scratch_shapes=[

time: 52.2 us -> 50.3 us (0.964)
  local copies, waits for them, and re-layouts: 1.87 us -> 0.8 us
  Pallas kernels: 50.1 us -> 49.3 us
    unnamed x1, local copies, waits for them, and re-layouts: 1.87 us -> 0.8 us
    pallas_call x1, Pallas kernels: 50.1 us -> 49.3 us  [shards(): pl.pallas_call(functools.partial(kernel, n_ctx, n_tp, group), out_shape=p...]
where the time goes in v4:
time: 50.3 us; the launch traced here: 50.1 us
  Pallas kernels  49.3 us (98%)
  local copies, waits for them, and re-layouts  0.8 us (2%)
    pallas_call x1, Pallas kernels, shards(): pl.pallas_call(functools.partial(kernel, n_ctx, n_tp, group), out_shape=p...  49.3 us

profile of v4, /device:TPU:4, one launch (start us, length us, event | category | flops | bytes accessed | tf_op | source)
XLA Modules:
  0.0 50.1 jit_solution(10182252934238037584)
XLA Ops:
  0.0 49.3 %shard_map.64 = bf16[256,1024]{1,0:T(8,128)(2,1)S(1)} custom-call(bf16[3,256,1024]{2,1,0:T(8,128)(2,1)} %bitcast.2, f32[3,3,1024]{2,1,0:T(4,128)} %taps.1, f32[16,64]{1,0:T(8,128)} %residues.1, f32[16,64]{1,0:T(8,128)} %rates.1, f32[1,1024]{1,0:T(1,128)} %bitcast.3, bf16[4096,1024]{1,0:T(8,128)(2,1)} %w_hbm.1), custom_call_target="tpu_custom_call" | custom-call | flops 2147483648 | bytes 8388608 | tf_op jit(solution)/shard_map/pallas_call | solution.py:376
  49.3 0.8 %copy.8 = bf16[256,1024]{1,0:T(8,128)(2,1)} copy(bf16[256,1024]{1,0:T(8,128)(2,1)S(1)} %shard_map.64) | data formatting | bytes 1048576

commit v5 on v4

--- a/solution.py
+++ b/solution.py
@@ -10,7 +10,7 @@
 MESH = pl.DeviceIdType.MESH
 LANES = 128
 SPAN = 64
-AHEAD = 3
+AHEAD = 4
 HALO = 16
 
 
@@ -124,7 +124,7 @@
         return 0
 
     ahead = min(AHEAD, blocks)
-    for b in range(ahead):
+    for b in range(ahead // 2):
         filters_of(b, 0)
     load.wait()
     w_copy.start()
@@ -199,6 +199,8 @@
         conv[b] = dot(filts[b], value, (1, 0))
         return 0
 
+    for b in range(ahead // 2, ahead):
+        filters_of(b, 0)
     for b in range(ahead):
         within(b, 0)
 
@@ -256,8 +258,8 @@
         return 0
 
     def both(b, _):
+        finish(b, 0)
         filters_of(b + ahead, 0)
-        finish(b, 0)
         within(b + ahead, 0)
         return 0
 

time: 50.3 us -> 50.1 us (level)
  no operation moved by 1% of the time
where the time goes in v5:
time: 50.1 us; the launch traced here: 50 us
  Pallas kernels  49.2 us (98%)
  local copies, waits for them, and re-layouts  0.8 us (2%)
    pallas_call x1, Pallas kernels, shards(): pl.pallas_call(functools.partial(kernel, n_ctx, n_tp, group), out_shape=p...  49.2 us

profile of v5, /device:TPU:4, one launch (start us, length us, event | category | flops | bytes accessed | tf_op | source)
XLA Modules:
  0.0 50.0 jit_solution(4601117740896671164)
XLA Ops:
  0.0 49.2 %shard_map.64 = bf16[256,1024]{1,0:T(8,128)(2,1)S(1)} custom-call(bf16[3,256,1024]{2,1,0:T(8,128)(2,1)} %bitcast.2, f32[3,3,1024]{2,1,0:T(4,128)} %taps.1, f32[16,64]{1,0:T(8,128)} %residues.1, f32[16,64]{1,0:T(8,128)} %rates.1, f32[1,1024]{1,0:T(1,128)} %bitcast.3, bf16[4096,1024]{1,0:T(8,128)(2,1)} %w_hbm.1), custom_call_target="tpu_custom_call" | custom-call | flops 2147483648 | bytes 8388608 | tf_op jit(solution)/shard_map/pallas_call | solution.py:378
  49.2 0.8 %copy.8 = bf16[256,1024]{1,0:T(8,128)(2,1)} copy(bf16[256,1024]{1,0:T(8,128)(2,1)S(1)} %shard_map.64) | data formatting | bytes 1048576
